TPU v7x, 32 devices: a whole 2x2x4 slice. The times are simulated.
32 devices in a mesh: pair: 4 (over y, x), virt: 8 (over z, core).
Axes of the slice: x: 2, y: 2, z: 4, core: 2. Of those that a mesh axis runs over, the one named last changes fastest.
Arguments:
- amplitudes: float32 [2048, 16384], P('pair', 'virt'), may hold values from -6 to 6
- integrals: bfloat16 [16384, 16384], P('pair', 'virt'), may hold values from -0.046875 to 0.046875
- occ_energy: float32 [2048], P('pair'), may hold values from 0.5 to 4
- vir_energy: float32 [16384], P('virt'), may hold values from 0.5 to 4
- tile_mask: int32 [256, 128], P('pair', 'virt'), may hold values 0 or 1
- partner_slot: int32 [256, 128], P('pair', 'virt'), may hold values from 0 to 31, as said below
Outputs:
- new_amplitudes: float32 [2048, 16384], P('pair', 'virt')
Inputs may be any that keep to these rules, and one draw needn't show every extreme that they name: `partner_slot`: within the block of tiles of each device (tile rows of one pair index by tile columns of one virt index), every device number 0 to 31 stands exactly 32 times, in an order drawn from the seed.
All inputs are finite; a program needn't handle non-finite values. No bound on the sum of `tile_mask` on one device may be relied on, other than what follows from the above.
Results may differ from a plain program's by a relative error of at most 0.0012.
Values may be sent and summed in bfloat16 or wider, within the bound.
A program may use at most 128 MiB of HBM per device.

v0:
```python
import jax
import jax.numpy as jnp
from jax import lax
from jax.sharding import PartitionSpec as P

TR = 8
TC = 128


def broadcast(value, axis, root):
    mine = lax.axis_index(axis) == root
    return lax.psum(jnp.where(mine, value, jnp.zeros_like(value)), axis)


def shards(amplitudes, integrals, occ_energy, vir_energy, tile_mask, partner_slot):
    row_count, col_count = amplitudes.shape
    amp_half = amplitudes.astype(jnp.bfloat16)
    pair_count = lax.axis_size("pair")
    virt_count = lax.axis_size("virt")
    all_rows = lax.all_gather(amp_half, "pair", axis=0, tiled=True)
    share = virt_count // pair_count
    pair_index = lax.axis_index("pair")
    owned = [broadcast(all_rows, "virt", pair_index * share + step) for step in range(share)]
    contraction = jnp.concatenate(owned, axis=1)
    ladder = lax.psum_scatter(
        jnp.dot(contraction, integrals, preferred_element_type=jnp.float32),
        "pair",
        scatter_dimension=0,
        tiled=True,
    )
    row_tiles = row_count // TR
    col_tiles = col_count // TC
    tile_total = row_tiles * col_tiles
    weights = tile_mask.astype(jnp.float32)
    masked = ladder.reshape(row_tiles, TR, col_tiles, TC) * weights[:, None, :, None]
    tiles = masked.transpose(0, 2, 1, 3).reshape(tile_total, TR * TC)
    slots = partner_slot.reshape(tile_total)
    ordering = jnp.argsort(slots, stable=True)
    inverse = jnp.argsort(ordering, stable=True)
    device_count = pair_count * virt_count
    per_peer = tile_total // device_count
    outgoing = jnp.take(tiles, ordering, axis=0)
    incoming = lax.all_to_all(
        outgoing.reshape(device_count, per_peer, TR * TC),
        ("pair", "virt"),
        split_axis=0,
        concat_axis=0,
        tiled=True,
    )
    partner = jnp.take(incoming.reshape(tile_total, TR * TC), inverse, axis=0)
    symmetric = (
        (tiles + partner)
        .reshape(row_tiles, col_tiles, TR, TC)
        .transpose(0, 2, 1, 3)
        .reshape(row_count, col_count)
    )
    denominator = occ_energy[:, None] + vir_energy[None, :]
    return amplitudes - symmetric / denominator


def solution(mesh):
    in_specs = (
        P("pair", "virt"),
        P("pair", "virt"),
        P("pair"),
        P("virt"),
        P("pair", "virt"),
        P("pair", "virt"),
    )
    out_specs = P("pair", "virt")
    return jax.shard_map(shards, mesh=mesh, in_specs=in_specs, out_specs=out_specs, check_vma=False)
```

profile of v0, /device:TPU:0, one launch (start us, length us, event | category | flops | bytes accessed | tf_op | source)
XLA Modules:
  0.0 786.8 jit_solution(6230717171035993540)
XLA Ops:
  6.5 3.8 convert_element_type.6
  10.4 90.4 %all-gather.2.cloned.1.call-done = bf16[2048,2048]{1,0:T(8,128)(2,1)} async-done(((bf16[512,2048]{1,0:T(8,128)(2,1)}), bf16[2048,2048]{1,0:T(8,128)(2,1)}) %all-gather.2.cloned.1.call-update) | async-done | bytes 8388624 | tf_op jit(solution)/shard_map/all_gather | solution.py:20
  100.9 9.5 %broadcast_select_fusion.1 = (bf16[2048,2048]{1,0:T(8,128)(2,1)}, bf16[2048,2048]{1,0:T(8,128)(2,1)}) fusion(bf16[2048,2048]{1,0:T(8,128)(2,1)} %all-gather.2.cloned.1.call-done, pred[]{:T(512)S(6)} %eq.6, pred[]{:T(512)S(6)} %eq.7), kind=kLoop, calls=%fused_computation.7 | loop fusion | flops 8388608 | bytes 25165826 | tf_op jit(solution)/shard_map/jit(_where)/select_n | solution.py:12
  110.3 0.0 reduce-scatter.2.cloned.1.call-start
  110.4 333.7 %all-reduce.3.cloned.1.call-done = (bf16[2048,2048]{1,0:T(8,128)(2,1)}, bf16[2048,2048]{1,0:T(8,128)(2,1)}) async-done(((bf16[2048,2048]{1,0:T(8,128)(2,1)}, bf16[2048,2048]{1,0:T(8,128)(2,1)}), (bf16[2048,2048]{1,0:T(8,128)(2,1)}, bf16[2048,2048]{1,0:T(8,128)(2,1)})) %all-reduce.3.cloned.1.call-update) | async-done | bytes 16777232 | tf_op jit(solution)/shard_map/psum | solution.py:12
  444.1 44.3 %fusion = f32[2048,2048]{1,0:T(8,128)} fusion(bf16[4096,2048]{1,0:T(8,128)(2,1)} %param.9, bf16[2048,2048]{1,0:T(8,128)(2,1)} %get-tuple-element.10, bf16[2048,2048]{1,0:T(8,128)(2,1)} %get-tuple-element.11), kind=kOutput, calls=%fused_computation.2 | convolution fusion | flops 34393292800 | bytes 50331648 | tf_op jit(solution)/shard_map/dot_general | solution.py:26
  488.4 0.7 copy-done.4
  489.1 0.1 copy.8
  489.1 0.1 copy.9
  489.2 0.1 reshape.31
  489.3 4.4 sort.31
  493.7 148.8 %reduce-scatter.2.cloned.1.call-done = f32[512,2048]{1,0:T(8,128)} async-done(((f32[2048,2048]{1,0:T(8,128)}), f32[512,2048]{1,0:T(8,128)}) %reduce-scatter.2.cloned.1.call-update) | async-done | bytes 4194320 | tf_op jit(solution)/shard_map/reduce_scatter | solution.py:25
  642.5 3.7 bitcast_multiply_fusion
  646.2 3.4 copy.15
  649.6 8.6 %gather_fusion = f32[1024,1024]{1,0:T(8,128)} fusion(f32[1024,1024]{1,0:T(8,128)} %bitcast.31, s32[1024]{0:T(1024)S(1)} %fusion.7), kind=kCustom, calls=%fused_computation.clone | custom fusion | bytes 8392704 | tf_op jit(solution)/shard_map/jit(_take)/gather | solution.py:42
  658.2 4.6 broadcast_select_fusion.2
  662.8 4.9 all-to-all-start
  667.7 4.4 sort.32
  672.1 90.5 %all-to-all-done = f32[32,32,1024]{2,1,0:T(8,128)} async-done(((f32[32,32,1024]{2,1,0:T(8,128)}), f32[32,32,1024]{2,1,0:T(8,128)}, u32[]{:S(2)}, u32[]{:S(2)}) %all-to-all-start) | async-done | bytes 4194336 | tf_op jit(solution)/shard_map/all_to_all | solution.py:43
  762.5 8.5 %gather_fusion.1 = f32[1024,1024]{1,0:T(8,128)} fusion(f32[1024,1024]{1,0:T(8,128)} %bitcast.3, s32[1024]{0:T(1024)S(1)} %fusion.8), kind=kCustom, calls=%fused_computation.1.clone | custom fusion | bytes 8392704 | tf_op jit(solution)/shard_map/jit(_take)/gather | solution.py:50
  771.1 4.4 fusion.6
  775.5 1.0 copy.11
  776.6 1.1 copy-done.1
  777.7 2.6 fusion.5
  (22 shorter events, 0.2 us)
Async XLA Ops:
  6.5 94.3 %all-gather.2.cloned.1.call-start = ((), (), s32[]{:S(2)}) async-start(), calls=%async_computation.2 | async-start | bytes 10485760 | tf_op jit(solution)/shard_map/all_gather | solution.py:20
  10.4 433.7 %all-reduce.3.cloned.1.call-start = ((), (), s32[]{:S(2)}) async-start(), calls=%async_computation.4 | async-start | bytes 33554432 | tf_op jit(solution)/shard_map/psum | solution.py:12
  110.3 532.2 %reduce-scatter.2.cloned.1.call-start = ((), (), s32[]{:S(2)}) async-start(), calls=%async_computation.3 | async-start | bytes 20971520 | tf_op jit(solution)/shard_map/reduce_scatter | solution.py:25
  488.4 0.7 copy-start.4
  488.4 0.8 copy-start.3
  646.2 3.4 copy-start
  662.8 99.8 %all-to-all-start = ((f32[32,32,1024]{2,1,0:T(8,128)}), f32[32,32,1024]{2,1,0:T(8,128)}, u32[]{:S(2)}, u32[]{:S(2)}) async-start(f32[32,32,1024]{2,1,0:T(8,128)} %bitcast.35), calls=%async_computation.1 | async-start | bytes 8388608 | tf_op jit(solution)/shard_map/all_to_all | solution.py:43
  775.5 2.2 copy-start.1
  775.5 2.2 copy-start.2
  775.5 2.2 copy-start.5
Sparse Core Ops, SparseCore 0:
  10.5 90.2 all-gather.1
  110.5 333.5 all-reduce.2
  488.5 153.9 reduce-scatter.1
where the time goes:
time: 787 us
  waiting for transfers between devices  663 us (84%)
  matrix products  44.3 us (6%)
  other arithmetic  37.3 us (5%)
  local copies, waits for them, and re-layouts  23.6 us (3%)
  between operations  13.2 us (2%)
    psum x1, waiting for transfers between devices, broadcast(): return lax.psum(jnp.where(mine, value, jnp.zeros_like(value)), axis)  334 us
    reduce_scatter x1, waiting for transfers between devices, shards(): lax.psum_scatter(jnp.dot(contraction, integrals, preferred_element_type=j...  149 us
    all_to_all x1, waiting for transfers between devices, shards(): lax.all_to_all(outgoing.reshape(device_count, per_peer, TR * TC), ('pair'...  90.5 us
    all_gather x1, waiting for transfers between devices, shards(): all_rows = lax.all_gather(amp_half, 'pair', axis=0, tiled=True)  90.4 us
    dot_general x1, matrix products, shards(): jnp.dot(contraction, integrals, preferred_element_type=jnp.float32)  44.3 us
  transfers between devices with their start and end apart: 4, of which 4 were waited for; matrix products, arithmetic and copies ran while one was open for 1% of the time, Pallas kernels for 0%

commit v1 on v0

v1 whole, which is shorter than its diff:
```python
import functools
import jax
import jax.numpy as jnp
from jax import lax
from jax.experimental import pallas as pl
from jax.experimental.pallas import tpu as pltpu
from jax.sharding import PartitionSpec as P

TR = 8
TC = 128
CHUNK = 64
LAG_CORE = 1
LAG_DOT = 2
LAG_SUM = 4
WIRE = jnp.bfloat16
TILE_WIRE = jnp.float16
MESH = pl.DeviceIdType.MESH


def ladder_kernel(
    pairs, virts, chunks, rows, tile_n,
    amp_ref, int_ref, out_ref, chain_ref,
    weights, gathered, part_out, part_in,
    weight_sem, chain_send, chain_recv, plane_send, plane_recv,
    core_send, core_recv, part_send, part_recv,
):
    share = virts // pairs
    spots = pairs
    p = lax.axis_index("pair")
    v = lax.axis_index("virt")
    u = v // share
    c = v % share
    depth = amp_ref.shape[1]
    width = int_ref.shape[1]

    load = pltpu.make_async_copy(int_ref, weights, weight_sem)
    load.start()

    barrier = pltpu.get_barrier_semaphore()

    def greet(pp, vv):
        pl.semaphore_signal(barrier, inc=1, device_id=(pp, vv), device_id_type=MESH)

    for k in range(1, pairs):
        greet((p + k) % pairs, v)
    for k in range(1, share):
        greet(p, u * share + (c + k) % share)

    for k in range(1, spots):
        greet(p, (u + k) % spots * share + c)

    pl.semaphore_wait(barrier, pairs - 1 + share - 1 + spots - 1)

    def piece(r):
        return pl.ds(pl.multiple_of(r * rows, rows), rows)

    def chain_copy(src, w, r, up):
        return pltpu.make_async_remote_copy(
            src_ref=src,
            dst_ref=chain_ref.at[w, piece(r)],
            send_sem=chain_send.at[up, w, r],
            recv_sem=chain_recv.at[w, r],
            device_id=(p, v + share if up else v - share),
            device_id_type=MESH,
        )

    def plane_copy(src, w, r):
        return pltpu.make_async_remote_copy(
            src_ref=src,
            dst_ref=gathered.at[c, r, p],
            send_sem=plane_send.at[w, r],
            recv_sem=plane_recv.at[p, r],
            device_id=(w, v),
            device_id_type=MESH,
        )

    def keep_copy(src, r):
        return pltpu.make_async_copy(src, gathered.at[c, r, p], plane_recv.at[p, r])

    def pass_on(src, w, r):
        @pl.when(w != p)
        def _():
            plane_copy(src, w, r).start()

        @pl.when(w == p)
        def _():
            keep_copy(src, r).start()

    def core_copy(k, r):
        return pltpu.make_async_remote_copy(
            src_ref=gathered.at[c, r],
            dst_ref=gathered.at[c, r],
            send_sem=core_send.at[k, r],
            recv_sem=core_recv.at[k, r],
            device_id=(p, u * share + (c + k) % share),
            device_id_type=MESH,
        )

    def part_copy(q, r):
        return pltpu.make_async_remote_copy(
            src_ref=part_out.at[r, q],
            dst_ref=part_in.at[r, p],
            send_sem=part_send.at[q, r],
            recv_sem=part_recv.at[p, r],
            device_id=(q, v),
            device_id_type=MESH,
        )

    def spread(r):
        mine = amp_ref.at[piece(r)]

        @pl.when(u > 0)
        def _():
            chain_copy(mine, u, r, 0).start()

        @pl.when(u < spots - 1)
        def _():
            chain_copy(mine, u, r, 1).start()

        pass_on(mine, u, r)
        for d in range(1, spots):
            low = u - d
            high = u + d

            @pl.when(low >= 0)
            def _():
                chain_copy(mine, low, r, 1).wait_recv()
                block = chain_ref.at[low, piece(r)]

                @pl.when(u < spots - 1)
                def _():
                    chain_copy(block, low, r, 1).start()

                pass_on(block, low, r)

            @pl.when(high < spots)
            def _():
                chain_copy(mine, high, r, 0).wait_recv()
                block = chain_ref.at[high, piece(r)]

                @pl.when(u > 0)
                def _():
                    chain_copy(block, high, r, 0).start()

                pass_on(block, high, r)

    def swap(r):
        keep_copy(amp_ref.at[piece(r)], r).wait()
        for k in range(1, pairs):
            q = (p + k) % pairs
            pltpu.make_async_remote_copy(
                src_ref=amp_ref.at[piece(r)],
                dst_ref=gathered.at[c, r, q],
                send_sem=plane_send.at[q, r],
                recv_sem=plane_recv.at[q, r],
                device_id=(q, v),
                device_id_type=MESH,
            ).wait_recv()
        for k in range(1, share):
            core_copy(k, r).start()

    def multiply(r):
        for k in range(1, share):
            pltpu.make_async_remote_copy(
                src_ref=gathered.at[c, r],
                dst_ref=gathered.at[(c + share - k) % share, r],
                send_sem=core_send.at[k, r],
                recv_sem=core_recv.at[k, r],
                device_id=(p, u * share + (c + share - k) % share),
                device_id_type=MESH,
            ).wait_recv()

        @pl.when(r == 0)
        def _():
            load.wait()

        def columns(n, carry):
            cut = pl.ds(pl.multiple_of(n * tile_n, tile_n), tile_n)
            total = jnp.zeros((pairs * rows, tile_n), jnp.float32)
            for s in range(share):
                total = total + jnp.dot(
                    gathered[s, r].reshape(pairs * rows, depth),
                    weights[s * depth : (s + 1) * depth, cut],
                    preferred_element_type=jnp.float32,
                )
            for q in range(pairs):
                part = total[q * rows : (q + 1) * rows]
                part_out[r, q, :, cut] = part.astype(WIRE)

                @pl.when(q == p)
                def _():
                    out_ref[piece(r), cut] = part
            return carry

        lax.fori_loop(0, width // tile_n, columns, 0)
        for k in range(1, pairs):
            part_copy((p + k) % pairs, r).start()

    def collect(r):
        for k in range(1, pairs):
            q = (p + k) % pairs
            pltpu.make_async_remote_copy(
                src_ref=part_out.at[r, q],
                dst_ref=part_in.at[r, q],
                send_sem=part_send.at[q, r],
                recv_sem=part_recv.at[q, r],
                device_id=(q, v),
                device_id_type=MESH,
            ).wait_recv()
        total = out_ref[piece(r), :]
        for k in range(1, pairs):
            total = total + part_in[r, (p + k) % pairs].astype(jnp.float32)
        out_ref[piece(r), :] = total

    def step(s, carry):
        @pl.when(s < chunks)
        def _():
            spread(s)

        @pl.when((s >= LAG_CORE) & (s < chunks + LAG_CORE))
        def _():
            swap(s - LAG_CORE)

        @pl.when((s >= LAG_DOT) & (s < chunks + LAG_DOT))
        def _():
            multiply(s - LAG_DOT)

        @pl.when(s >= LAG_SUM)
        def _():
            collect(s - LAG_SUM)

        return carry

    lax.fori_loop(0, chunks + LAG_SUM, step, 0)

    def drain(r, carry):
        mine = amp_ref.at[piece(r)]
        for w in range(spots):
            @pl.when((u > 0) & (w >= u))
            def _():
                chain_copy(mine, w, r, 0).wait_send()

            @pl.when((u < spots - 1) & (w <= u))
            def _():
                chain_copy(mine, w, r, 1).wait_send()

            @pl.when(w != p)
            def _():
                plane_copy(mine, w, r).wait_send()
                part_copy(w, r).wait_send()
        for k in range(1, share):
            core_copy(k, r).wait_send()
        return carry

    lax.fori_loop(0, chunks, drain, 0)


def ladder_block(amp_half, integrals, pairs, virts):
    row_count, depth = amp_half.shape
    width = integrals.shape[1]
    rows = min(CHUNK, row_count)
    chunks = row_count // rows
    share = virts // pairs
    tile_n = min(256, width)
    dma = pltpu.SemaphoreType.DMA
    ladder, _ = pl.pallas_call(
        functools.partial(ladder_kernel, pairs, virts, chunks, rows, tile_n),
        out_shape=(
            jax.ShapeDtypeStruct((row_count, width), jnp.float32),
            jax.ShapeDtypeStruct((pairs, row_count, depth), jnp.bfloat16),
        ),
        in_specs=[pl.BlockSpec(memory_space=pl.ANY)] * 2,
        out_specs=(
            pl.BlockSpec(memory_space=pltpu.VMEM),
            pl.BlockSpec(memory_space=pl.ANY),
        ),
        scratch_shapes=[
            pltpu.VMEM(integrals.shape, jnp.bfloat16),
            pltpu.VMEM((share, chunks, pairs, rows, depth), jnp.bfloat16),
            pltpu.VMEM((chunks, pairs, rows, width), WIRE),
            pltpu.VMEM((chunks, pairs, rows, width), WIRE),
            dma(()),
            dma((2, pairs, chunks)),
            dma((pairs, chunks)),
            dma((pairs, chunks)),
            dma((pairs, chunks)),
            dma((share, chunks)),
            dma((share, chunks)),
            dma((pairs, chunks)),
            dma((pairs, chunks)),
        ],
        compiler_params=pltpu.CompilerParams(
            collective_id=0, has_side_effects=True, vmem_limit_bytes=60 * 2**20
        ),
        cost_estimate=pl.CostEstimate(
            flops=2 * pairs * row_count * share * depth * width,
            bytes_accessed=2 * integrals.size + 8 * amp_half.size,
            transcendentals=0,
        ),
    )(amp_half, integrals)
    return ladder


def shards(amplitudes, integrals, occ_energy, vir_energy, tile_mask, partner_slot):
    row_count, col_count = amplitudes.shape
    pair_count = lax.axis_size("pair")
    virt_count = lax.axis_size("virt")
    ladder = ladder_block(amplitudes.astype(jnp.bfloat16), integrals, pair_count, virt_count)
    row_tiles = row_count // TR
    col_tiles = col_count // TC
    tile_total = row_tiles * col_tiles
    device_count = pair_count * virt_count
    per_peer = tile_total // device_count
    slots = partner_slot.reshape(tile_total)
    place = jnp.arange(tile_total, dtype=jnp.int32)
    earlier = (slots[None, :] == slots[:, None]) & (place[None, :] < place[:, None])
    inverse = slots * per_peer + jnp.sum(earlier.astype(jnp.int32), axis=1)
    hit = inverse[None, :] == place[:, None]
    ordering = jnp.sum(jnp.where(hit, place[None, :], 0), axis=1)
    weights = tile_mask.astype(jnp.float32)
    masked = ladder.reshape(row_tiles, TR, col_tiles, TC) * weights[:, None, :, None]
    tiles = masked.transpose(0, 2, 1, 3).reshape(tile_total, TR * TC)
    outgoing = jnp.take(tiles.astype(TILE_WIRE), ordering, axis=0)
    incoming = lax.all_to_all(
        outgoing.reshape(device_count, per_peer, TR * TC),
        ("pair", "virt"),
        split_axis=0,
        concat_axis=0,
        tiled=True,
    )
    partner = jnp.take(incoming.reshape(tile_total, TR * TC), inverse, axis=0)
    symmetric = (
        (tiles + partner.astype(jnp.float32))
        .reshape(row_tiles, col_tiles, TR, TC)
        .transpose(0, 2, 1, 3)
        .reshape(row_count, col_count)
    )
    denominator = occ_energy[:, None] + vir_energy[None, :]
    return amplitudes - symmetric / denominator


def solution(mesh):
    in_specs = (
        P("pair", "virt"),
        P("pair", "virt"),
        P("pair"),
        P("virt"),
        P("pair", "virt"),
        P("pair", "virt"),
    )
    out_specs = P("pair", "virt")
    return jax.shard_map(shards, mesh=mesh, in_specs=in_specs, out_specs=out_specs, check_vma=False)
```

time: 787 us -> 324 us (0.41)
  waiting for transfers between devices: 663 us -> 50.1 us
  Pallas kernels: 0 us -> 233 us
  matrix products: 44.3 us -> 0 us
  other arithmetic: 37.3 us -> 19.3 us
  between operations: 13.2 us -> 0.11 us
  local copies, waits for them, and re-layouts: 23.6 us -> 15.4 us
    psum x1 -> x0, waiting for transfers between devices: 334 us -> none  [broadcast(): return lax.psum(jnp.where(mine, value, jnp.zeros_like(value)), axis)]
    pallas_call x0 -> x1, Pallas kernels: none -> 233 us  [ladder_block(): pl.pallas_call(functools.partial(ladder_kernel, pairs, virts, chunks, row...]
    reduce_scatter x1 -> x0, waiting for transfers between devices: 149 us -> none  [shards(): lax.psum_scatter(jnp.dot(contraction, integrals, preferred_element_type=j...]
    all_gather x1 -> x0, waiting for transfers between devices: 90.4 us -> none  [shards(): all_rows = lax.all_gather(amp_half, 'pair', axis=0, tiled=True)]
    dot_general x1 -> x0, matrix products: 44.3 us -> none  [shards(): jnp.dot(contraction, integrals, preferred_element_type=jnp.float32)]
    all_to_all x1, waiting for transfers between devices: 90.5 us -> 50.1 us  [shards(): lax.all_to_all(outgoing.reshape(device_count, per_peer, TR * TC), ('pair'...]
    select_n x2 -> x1, other arithmetic: 14 us -> 3.47 us  [shards(): outgoing = jnp.take(tiles.astype(TILE_WIRE), ordering, axis=0)]
    sort x2 -> x0, other arithmetic: 8.74 us -> none  [the longest x1 4.37 us: shards(): ordering = jnp.argsort(slots, stable=True)]
  transfers between devices with their start and end apart: 4 -> 1, of which waited for: 4 -> 1; matrix products, arithmetic and copies ran while one was open for 1% -> 0% of each run, Pallas kernels for 0% -> 0%
where the time goes in v1:
time: 324 us; the launch traced here: 323 us
  Pallas kernels  233 us (72%)
  waiting for transfers between devices  50.1 us (15%)
  other arithmetic  19.3 us (6%)
  local copies, waits for them, and re-layouts  15.4 us (5%)
  starting transfers between devices  5.1 us (2%)
    pallas_call x1, Pallas kernels, ladder_block(): pl.pallas_call(functools.partial(ladder_kernel, pairs, virts, chunks, row...  233 us
    all_to_all x1, waiting for transfers between devices, shards(): lax.all_to_all(outgoing.reshape(device_count, per_peer, TR * TC), ('pair'...  50.1 us
  transfers between devices with their start and end apart: 1, of which 1 were waited for; matrix products, arithmetic and copies ran while one was open for 0% of the time, Pallas kernels for 0%

profile of v1, /device:TPU:0, one launch (start us, length us, event | category | flops | bytes accessed | tf_op | source)
XLA Modules:
  0.0 323.5 jit_solution(12035007501633076653)
XLA Ops:
  0.0 0.8 copy.11
  0.8 0.1 reshape.41
  0.9 0.5 convert_reduce_fusion
  1.4 0.5 select_reduce_fusion
  1.9 3.8 %convert_element_type.15.amp_ref = bf16[512,2048]{1,0:T(8,128)(2,1)} convert(f32[512,2048]{1,0:T(8,128)} %param.8) | non-fusion elementwise | flops 1048576 | bytes 6291456 | tf_op jit(solution)/shard_map/convert_element_type | solution.py:308
  5.8 0.0 copy-done.3
  5.8 0.1 copy.10
  5.9 233.5 %shard_map.64 = (f32[512,2048]{1,0:T(8,128)}, bf16[4,512,2048]{2,1,0:T(8,128)(2,1)}) custom-call(bf16[512,2048]{1,0:T(8,128)(2,1)} %convert_element_type.15.amp_ref, bf16[4096,2048]{1,0:T(8,128)(2,1)} %int_ref.1), custom_call_target="tpu_custom_call" | custom-call | flops 34359738368 | bytes 25165824 | tf_op jit(solution)/shard_map/pallas_call | solution.py:266
  239.3 3.7 %bitcast_multiply_fusion = f32[64,8,16,128]{3,1,2,0:T(8,128)S(1)} fusion(f32[512,2048]{1,0:T(8,128)} %get-tuple-element.7, f32[64,16]{1,0:T(8,128)S(1)} %copy.10), kind=kLoop, calls=%fused_computation.8 | loop fusion | flops 1048576 | bytes 8392704 | tf_op jit(solution)/shard_map/mul | solution.py:321
  243.0 0.0 copy-start
  243.0 2.0 copy-done
  245.0 0.8 bitcast_convert_fusion
  245.8 5.1 %gather_fusion = f16[1024,1024]{1,0:T(8,128)(2,1)} fusion(f16[1024,1024]{1,0:T(8,128)(2,1)S(1)} %bitcast_convert_fusion, s32[1024]{0:T(1024)S(1)} %fusion.4), kind=kCustom, calls=%fused_computation.clone | custom fusion | bytes 4198400 | tf_op jit(solution)/shard_map/jit(_take)/gather | solution.py:323
  251.0 3.5 %broadcast_select_fusion = f16[1024,1024]{1,0:T(8,128)(2,1)} fusion(f16[1024,1024]{1,0:T(8,128)(2,1)} %gather_fusion, pred[1024]{0:T(1024)(128)(4,1)S(1)} %compare_and_fusion.1), kind=kLoop, calls=%fused_computation.14 | loop fusion | flops 1048576 | bytes 4195328 | tf_op jit(solution)/shard_map/jit(_take)/select_n | solution.py:323
  254.5 5.1 %all-to-all-start = ((f16[32,32,1024]{2,1,0:T(8,128)(2,1)}), f16[32,32,1024]{2,1,0:T(8,128)(2,1)S(1)}, u32[]{:S(2)}, u32[]{:S(2)}) async-start(f16[32,32,1024]{2,1,0:T(8,128)(2,1)} %bitcast.34), calls=%async_computation | async-start | bytes 4194304 | tf_op jit(solution)/shard_map/all_to_all | solution.py:324
  259.6 50.1 %all-to-all-done = f16[32,32,1024]{2,1,0:T(8,128)(2,1)S(1)} async-done(((f16[32,32,1024]{2,1,0:T(8,128)(2,1)}), f16[32,32,1024]{2,1,0:T(8,128)(2,1)S(1)}, u32[]{:S(2)}, u32[]{:S(2)}) %all-to-all-start) | async-done | bytes 2097184 | tf_op jit(solution)/shard_map/all_to_all | solution.py:324
  309.7 5.1 %gather_fusion.1 = f16[1024,1024]{1,0:T(8,128)(2,1)} fusion(f16[1024,1024]{1,0:T(8,128)(2,1)S(1)} %bitcast.30, s32[1024]{0:T(1024)S(1)} %fusion.5), kind=kCustom, calls=%fused_computation.1.clone | custom fusion | bytes 4198400 | tf_op jit(solution)/shard_map/jit(_take)/gather | solution.py:331
  314.8 3.8 %fusion.2 = f32[128,8,8,128]{3,1,2,0:T(8,128)S(1)} fusion(f32[128,8,8,128]{3,2,1,0:T(8,128)} %bitcast.32, f16[1024,1024]{1,0:T(8,128)(2,1)} %gather_fusion.1, pred[1024]{0:T(1024)(128)(4,1)S(1)} %get-tuple-element.8), kind=kLoop, calls=%fused_computation.7 | loop fusion | flops 3145728 | bytes 10486784
  318.7 0.0 copy-start.1
  318.7 0.0 copy-start.2
  318.7 0.0 copy-start.4
  318.7 1.0 copy.13
  319.7 1.1 copy-done.1
  320.9 2.6 fusion.1
  (8 shorter events, 0.0 us)
Async XLA Ops:
  0.0 5.8 %copy-start.3 = (s32[64,16]{0,1:T(8,128)S(1)}, s32[64,16]{0,1:T(8,128)}, u32[]{:S(2)}) copy-start(s32[64,16]{0,1:T(8,128)} %param.12) | copy-start | bytes 12292
  243.0 2.0 copy-start
  254.5 55.2 %all-to-all-start = ((f16[32,32,1024]{2,1,0:T(8,128)(2,1)}), f16[32,32,1024]{2,1,0:T(8,128)(2,1)S(1)}, u32[]{:S(2)}, u32[]{:S(2)}) async-start(f16[32,32,1024]{2,1,0:T(8,128)(2,1)} %bitcast.34), calls=%async_computation | async-start | bytes 4194304 | tf_op jit(solution)/shard_map/all_to_all | solution.py:324
  318.7 2.2 copy-start.1
  318.7 2.2 copy-start.2
  318.7 2.2 copy-start.4

commit v2 on v1

--- a/solution.py
+++ b/solution.py
@@ -8,11 +8,13 @@
 
 TR = 8
 TC = 128
-CHUNK = 64
+CHUNK = 32
 LAG_CORE = 1
 LAG_DOT = 2
 LAG_SUM = 4
-WIRE = jnp.bfloat16
+WIRE = jnp.int16
+TOP = 32767
+BOUND = 6.0 * 0.046875
 TILE_WIRE = jnp.float16
 MESH = pl.DeviceIdType.MESH
 
@@ -20,7 +22,7 @@
 def ladder_kernel(
     pairs, virts, chunks, rows, tile_n,
     amp_ref, int_ref, out_ref, chain_ref,
-    weights, gathered, part_out, part_in,
+    weights, gathered, part_out, part_in, product,
     weight_sem, chain_send, chain_recv, plane_send, plane_recv,
     core_send, core_recv, part_send, part_recv,
 ):
@@ -174,7 +176,7 @@
         def _():
             load.wait()
 
-        def columns(n, carry):
+        def columns(n, top):
             cut = pl.ds(pl.multiple_of(n * tile_n, tile_n), tile_n)
             total = jnp.zeros((pairs * rows, tile_n), jnp.float32)
             for s in range(share):
@@ -183,16 +185,32 @@
                     weights[s * depth : (s + 1) * depth, cut],
                     preferred_element_type=jnp.float32,
                 )
+            product[:, cut] = total
+            for g in range(0, tile_n, TC):
+                top = jnp.maximum(top, jnp.abs(total[:, g : g + TC]))
+            return top
+
+        top = lax.fori_loop(
+            0, width // tile_n, columns, jnp.zeros((pairs * rows, TC), jnp.float32)
+        )
+        bound = share * depth * BOUND
+        top = jnp.max(top, axis=1, keepdims=True)
+        scale = jnp.clip(jnp.floor(top * (TOP / bound)) + 1.0, 1.0, float(TOP))
+        inverse = (TOP * (TOP / bound)) / scale
+        codes = jnp.broadcast_to(scale, (pairs * rows, TC)).astype(jnp.int32).astype(WIRE)
+        for q in range(pairs):
+            part_out[r, q, :, width:] = codes[q * rows : (q + 1) * rows]
+
+        def encode(n, carry):
+            cut = pl.ds(pl.multiple_of(n * tile_n, tile_n), tile_n)
+            code = jnp.floor(product[:, cut] * inverse + 0.5)
+            code = jnp.clip(code, -float(TOP), float(TOP)).astype(jnp.int32).astype(WIRE)
             for q in range(pairs):
-                part = total[q * rows : (q + 1) * rows]
-                part_out[r, q, :, cut] = part.astype(WIRE)
-
-                @pl.when(q == p)
-                def _():
-                    out_ref[piece(r), cut] = part
+                part_out[r, q, :, cut] = code[q * rows : (q + 1) * rows]
             return carry
 
-        lax.fori_loop(0, width // tile_n, columns, 0)
+        lax.fori_loop(0, width // tile_n, encode, 0)
+        out_ref[piece(r), :] = product[pl.ds(pl.multiple_of(p * rows, rows), rows), :]
         for k in range(1, pairs):
             part_copy((p + k) % pairs, r).start()
 
@@ -207,9 +225,13 @@
                 device_id=(q, v),
                 device_id_type=MESH,
             ).wait_recv()
+        unit = share * depth * BOUND / TOP / TOP
         total = out_ref[piece(r), :]
         for k in range(1, pairs):
-            total = total + part_in[r, (p + k) % pairs].astype(jnp.float32)
+            q = (p + k) % pairs
+            scale = part_in[r, q, :, width:].astype(jnp.int32).astype(jnp.float32)[:, :1]
+            code = part_in[r, q, :, :width].astype(jnp.int32).astype(jnp.float32)
+            total = total + code * (scale * unit)
         out_ref[piece(r), :] = total
 
     def step(s, carry):
@@ -277,8 +299,9 @@
         scratch_shapes=[
             pltpu.VMEM(integrals.shape, jnp.bfloat16),
             pltpu.VMEM((share, chunks, pairs, rows, depth), jnp.bfloat16),
-            pltpu.VMEM((chunks, pairs, rows, width), WIRE),
-            pltpu.VMEM((chunks, pairs, rows, width), WIRE),
+            pltpu.VMEM((chunks, pairs, rows, width + TC), WIRE),
+            pltpu.VMEM((chunks, pairs, rows, width + TC), WIRE),
+            pltpu.VMEM((pairs * rows, width), jnp.float32),
             dma(()),
             dma((2, pairs, chunks)),
             dma((pairs, chunks)),

time: 324 us -> 416 us (1.28)
  Pallas kernels: 233 us -> 328 us
    pallas_call x1, Pallas kernels: 233 us -> 328 us  [ladder_block(): pl.pallas_call(functools.partial(ladder_kernel, pairs, virts, chunks, row...]
where the time goes in v2:
time: 416 us
  Pallas kernels  328 us (79%)
  waiting for transfers between devices  50.1 us (12%)
  other arithmetic  19.3 us (5%)
  local copies, waits for them, and re-layouts  15.4 us (4%)
    pallas_call x1, Pallas kernels, ladder_block(): pl.pallas_call(functools.partial(ladder_kernel, pairs, virts, chunks, row...  328 us
    all_to_all x1, waiting for transfers between devices, shards(): lax.all_to_all(outgoing.reshape(device_count, per_peer, TR * TC), ('pair'...  50.1 us
  transfers between devices with their start and end apart: 1, of which 1 were waited for; matrix products, arithmetic and copies ran while one was open for 0% of the time, Pallas kernels for 0%

profile of v2, /device:TPU:0, one launch (start us, length us, event | category | flops | bytes accessed | tf_op | source)
XLA Modules:
  0.0 415.5 jit_solution(13154466843282068834)
XLA Ops:
  0.0 0.8 copy.11
  0.8 0.1 reshape.41
  0.9 0.5 convert_reduce_fusion
  1.4 0.5 select_reduce_fusion
  1.9 3.8 convert_element_type.15.amp_ref
  5.8 0.0 copy-done.3
  5.8 0.1 copy.10
  5.9 327.9 %shard_map.64 = (f32[512,2048]{1,0:T(8,128)}, bf16[4,512,2048]{2,1,0:T(8,128)(2,1)}) custom-call(bf16[512,2048]{1,0:T(8,128)(2,1)} %convert_element_type.15.amp_ref, bf16[4096,2048]{1,0:T(8,128)(2,1)} %int_ref.1), custom_call_target="tpu_custom_call" | custom-call | flops 34359738368 | bytes 25165824 | tf_op jit(solution)/shard_map/pallas_call | solution.py:288
  333.7 3.7 bitcast_multiply_fusion
  337.4 0.0 copy-start
  337.4 2.0 copy-done
  339.4 0.8 bitcast_convert_fusion
  340.3 5.1 %gather_fusion = f16[1024,1024]{1,0:T(8,128)(2,1)} fusion(f16[1024,1024]{1,0:T(8,128)(2,1)S(1)} %bitcast_convert_fusion, s32[1024]{0:T(1024)S(1)} %fusion.4), kind=kCustom, calls=%fused_computation.clone | custom fusion | bytes 4198400 | tf_op jit(solution)/shard_map/jit(_take)/gather | solution.py:346
  345.4 3.5 broadcast_select_fusion
  348.9 2.7 all-to-all-start
  351.6 50.1 %all-to-all-done = f16[32,32,1024]{2,1,0:T(8,128)(2,1)S(1)} async-done(((f16[32,32,1024]{2,1,0:T(8,128)(2,1)}), f16[32,32,1024]{2,1,0:T(8,128)(2,1)S(1)}, u32[]{:S(2)}, u32[]{:S(2)}) %all-to-all-start) | async-done | bytes 2097184 | tf_op jit(solution)/shard_map/all_to_all | solution.py:347
  401.7 5.1 %gather_fusion.1 = f16[1024,1024]{1,0:T(8,128)(2,1)} fusion(f16[1024,1024]{1,0:T(8,128)(2,1)S(1)} %bitcast.30, s32[1024]{0:T(1024)S(1)} %fusion.5), kind=kCustom, calls=%fused_computation.1.clone | custom fusion | bytes 4198400 | tf_op jit(solution)/shard_map/jit(_take)/gather | solution.py:354
  406.8 3.8 fusion.2
  410.7 0.0 copy-start.1
  410.7 0.0 copy-start.2
  410.7 0.0 copy-start.4
  410.7 1.0 copy.13
  411.8 1.1 copy-done.1
  412.9 2.6 fusion.1
  (8 shorter events, 0.0 us)
Async XLA Ops:
  0.0 5.8 %copy-start.3 = (s32[64,16]{0,1:T(8,128)S(1)}, s32[64,16]{0,1:T(8,128)}, u32[]{:S(2)}) copy-start(s32[64,16]{0,1:T(8,128)} %param.12) | copy-start | bytes 12292
  337.4 2.0 copy-start
  348.9 52.8 %all-to-all-start = ((f16[32,32,1024]{2,1,0:T(8,128)(2,1)}), f16[32,32,1024]{2,1,0:T(8,128)(2,1)S(1)}, u32[]{:S(2)}, u32[]{:S(2)}) async-start(f16[32,32,1024]{2,1,0:T(8,128)(2,1)} %bitcast.34), calls=%async_computation | async-start | bytes 4194304 | tf_op jit(solution)/shard_map/all_to_all | solution.py:347
  410.7 2.2 copy-start.1
  410.7 2.2 copy-start.2
  410.7 2.2 copy-start.4

commit v3 on v2

--- a/solution.py
+++ b/solution.py
@@ -8,10 +8,10 @@
 
 TR = 8
 TC = 128
-CHUNK = 32
+CHUNK = 128
 LAG_CORE = 1
 LAG_DOT = 2
-LAG_SUM = 4
+LAG_SUM = 3
 WIRE = jnp.int16
 TOP = 32767
 BOUND = 6.0 * 0.046875

time: 416 us -> 344 us (0.83)
  Pallas kernels: 328 us -> 241 us
  starting transfers between devices: 2.73 us -> 17.5 us
    pallas_call x1, Pallas kernels: 328 us -> 241 us  [ladder_block(): pl.pallas_call(functools.partial(ladder_kernel, pairs, virts, chunks, row...]
    all_to_all x1, starting transfers between devices: 2.73 us -> 17.5 us  [shards(): lax.all_to_all(outgoing.reshape(device_count, per_peer, TR * TC), ('pair'...]
where the time goes in v3:
time: 344 us
  Pallas kernels  241 us (70%)
  waiting for transfers between devices  50.1 us (15%)
  other arithmetic  19.3 us (6%)
  starting transfers between devices  17.5 us (5%)
  local copies, waits for them, and re-layouts  15.4 us (4%)
    pallas_call x1, Pallas kernels, ladder_block(): pl.pallas_call(functools.partial(ladder_kernel, pairs, virts, chunks, row...  241 us
    all_to_all x1, waiting for transfers between devices, shards(): lax.all_to_all(outgoing.reshape(device_count, per_peer, TR * TC), ('pair'...  50.1 us
    all_to_all x1, starting transfers between devices, shards(): lax.all_to_all(outgoing.reshape(device_count, per_peer, TR * TC), ('pair'...  17.5 us
  transfers between devices with their start and end apart: 1, of which 1 were waited for; matrix products, arithmetic and copies ran while one was open for 0% of the time, Pallas kernels for 0%

profile of v3, /device:TPU:0, one launch (start us, length us, event | category | flops | bytes accessed | tf_op | source)
XLA Modules:
  0.0 343.8 jit_solution(7048352664734109697)
XLA Ops:
  0.0 0.8 copy.11
  0.8 0.1 reshape.41
  0.9 0.5 convert_reduce_fusion
  1.4 0.5 select_reduce_fusion
  1.9 3.8 %convert_element_type.15.amp_ref = bf16[512,2048]{1,0:T(8,128)(2,1)} convert(f32[512,2048]{1,0:T(8,128)} %param.8) | non-fusion elementwise | flops 1048576 | bytes 6291456 | tf_op jit(solution)/shard_map/convert_element_type | solution.py:331
  5.8 0.0 copy-done.3
  5.8 0.1 copy.10
  5.9 241.4 %shard_map.64 = (f32[512,2048]{1,0:T(8,128)}, bf16[4,512,2048]{2,1,0:T(8,128)(2,1)}) custom-call(bf16[512,2048]{1,0:T(8,128)(2,1)} %convert_element_type.15.amp_ref, bf16[4096,2048]{1,0:T(8,128)(2,1)} %int_ref.1), custom_call_target="tpu_custom_call" | custom-call | flops 34359738368 | bytes 25165824 | tf_op jit(solution)/shard_map/pallas_call | solution.py:288
  247.2 3.7 %bitcast_multiply_fusion = f32[64,8,16,128]{3,1,2,0:T(8,128)S(1)} fusion(f32[512,2048]{1,0:T(8,128)} %get-tuple-element.7, f32[64,16]{1,0:T(8,128)S(1)} %copy.10), kind=kLoop, calls=%fused_computation.8 | loop fusion | flops 1048576 | bytes 8392704 | tf_op jit(solution)/shard_map/mul | solution.py:344
  250.9 0.0 copy-start
  250.9 2.0 copy-done
  252.9 0.8 bitcast_convert_fusion
  253.7 5.1 %gather_fusion = f16[1024,1024]{1,0:T(8,128)(2,1)} fusion(f16[1024,1024]{1,0:T(8,128)(2,1)S(1)} %bitcast_convert_fusion, s32[1024]{0:T(1024)S(1)} %fusion.4), kind=kCustom, calls=%fused_computation.clone | custom fusion | bytes 4198400 | tf_op jit(solution)/shard_map/jit(_take)/gather | solution.py:346
  258.9 3.5 %broadcast_select_fusion = f16[1024,1024]{1,0:T(8,128)(2,1)} fusion(f16[1024,1024]{1,0:T(8,128)(2,1)} %gather_fusion, pred[1024]{0:T(1024)(128)(4,1)S(1)} %compare_and_fusion.1), kind=kLoop, calls=%fused_computation.14 | loop fusion | flops 1048576 | bytes 4195328 | tf_op jit(solution)/shard_map/jit(_take)/select_n | solution.py:346
  262.4 17.5 %all-to-all-start = ((f16[32,32,1024]{2,1,0:T(8,128)(2,1)}), f16[32,32,1024]{2,1,0:T(8,128)(2,1)S(1)}, u32[]{:S(2)}, u32[]{:S(2)}) async-start(f16[32,32,1024]{2,1,0:T(8,128)(2,1)} %bitcast.34), calls=%async_computation | async-start | bytes 4194304 | tf_op jit(solution)/shard_map/all_to_all | solution.py:347
  279.9 50.1 %all-to-all-done = f16[32,32,1024]{2,1,0:T(8,128)(2,1)S(1)} async-done(((f16[32,32,1024]{2,1,0:T(8,128)(2,1)}), f16[32,32,1024]{2,1,0:T(8,128)(2,1)S(1)}, u32[]{:S(2)}, u32[]{:S(2)}) %all-to-all-start) | async-done | bytes 2097184 | tf_op jit(solution)/shard_map/all_to_all | solution.py:347
  330.0 5.1 %gather_fusion.1 = f16[1024,1024]{1,0:T(8,128)(2,1)} fusion(f16[1024,1024]{1,0:T(8,128)(2,1)S(1)} %bitcast.30, s32[1024]{0:T(1024)S(1)} %fusion.5), kind=kCustom, calls=%fused_computation.1.clone | custom fusion | bytes 4198400 | tf_op jit(solution)/shard_map/jit(_take)/gather | solution.py:354
  335.1 3.8 %fusion.2 = f32[128,8,8,128]{3,1,2,0:T(8,128)S(1)} fusion(f32[128,8,8,128]{3,2,1,0:T(8,128)} %bitcast.32, f16[1024,1024]{1,0:T(8,128)(2,1)} %gather_fusion.1, pred[1024]{0:T(1024)(128)(4,1)S(1)} %get-tuple-element.8), kind=kLoop, calls=%fused_computation.7 | loop fusion | flops 3145728 | bytes 10486784
  338.9 0.0 copy-start.1
  339.0 0.0 copy-start.2
  339.0 0.0 copy-start.4
  339.0 1.0 copy.13
  340.0 1.1 copy-done.1
  341.1 2.6 fusion.1
  (8 shorter events, 0.0 us)
Async XLA Ops:
  0.0 5.8 %copy-start.3 = (s32[64,16]{0,1:T(8,128)S(1)}, s32[64,16]{0,1:T(8,128)}, u32[]{:S(2)}) copy-start(s32[64,16]{0,1:T(8,128)} %param.12) | copy-start | bytes 12292
  250.9 2.0 copy-start
  262.4 67.6 %all-to-all-start = ((f16[32,32,1024]{2,1,0:T(8,128)(2,1)}), f16[32,32,1024]{2,1,0:T(8,128)(2,1)S(1)}, u32[]{:S(2)}, u32[]{:S(2)}) async-start(f16[32,32,1024]{2,1,0:T(8,128)(2,1)} %bitcast.34), calls=%async_computation | async-start | bytes 4194304 | tf_op jit(solution)/shard_map/all_to_all | solution.py:347
  338.9 2.2 copy-start.1
  339.0 2.2 copy-start.2
  339.0 2.2 copy-start.4
